TPU v7x, 256 devices: a whole 4x4x8 slice. The times are simulated.
256 devices in a mesh: section: 64 (over x, y_hi, z), tensor: 4 (over y_lo, core).
Axes of the slice: x: 4, y: 4 (y_hi: 2, y_lo: 2; y = y_hi * 2 + y_lo), z: 8, core: 2. Of those that a mesh axis runs over, the one named last changes fastest.
Arguments:
- state: bfloat16 [64, 16, 2560], P('section'), may hold values from -6 to 6
- gain_in: bfloat16 [64, 2560], P('section'), may hold values from 0.25 to 1.75
- w_query: bfloat16 [64, 2560, 4096], P('section', None, 'tensor'), may hold values from -0.125 to 0.125
- w_key: bfloat16 [64, 2560, 512], P('section', None, 'tensor'), may hold values from -0.125 to 0.125
- w_value: bfloat16 [64, 2560, 512], P('section', None, 'tensor'), may hold values from -0.125 to 0.125
- w_output: bfloat16 [64, 4096, 2560], P('section', 'tensor'), may hold values from -0.375 to 0.375
- query_gain: bfloat16 [64, 128], P('section'), may hold values from 0.099609375 to 1.8984375
- key_gain: bfloat16 [64, 128], P('section'), may hold values from 0.099609375 to 1.8984375
- cache_keys: bfloat16 [64, 16, 4, 32, 128], P('section', None, 'tensor'), may hold values from -600 to 600
- cache_values: bfloat16 [64, 16, 4, 32, 128], P('section', None, 'tensor'), may hold values from -6 to 6
- lengths: int32 [64, 16], P('section'), may hold values from 4 to 32, as said below
Outputs:
- handed: bfloat16 [64, 16, 2560], P('section')
- new_keys: bfloat16 [64, 16, 4, 128], P('section', None, 'tensor')
- new_values: bfloat16 [64, 16, 4, 128], P('section', None, 'tensor')
Inputs may be any that keep to these rules, and one draw needn't show every extreme that they name: `lengths`: in every section at least one row holds 32 tokens.
All inputs are finite; a program needn't handle non-finite values.
Results may differ from a plain program's by a relative error of at most 0.012.
The roundings to bfloat16 on the way count: a program that leaves them out, or rounds other values in their place, can miss the bound.
Values may be sent and summed in bfloat16 or wider, within the bound.
No kernel may reach another device: no remote copies, remote signals or barrier semaphores. Data moves between devices by JAX's collectives and lax.ppermute only.
A program may use at most 64 MiB of HBM per device.

v0:
```python
import jax
import jax.numpy as jnp
from jax import lax
from jax.sharding import PartitionSpec as P

HD = 128


epsilon = 1e-06
rope_base = 1000000.0


def shifted(value, axis, steps):
    count = lax.axis_size(axis)
    pairs = [(source, (source + steps) % count) for source in range(count)]
    return lax.ppermute(value, axis, pairs)


def rms_norm(values, gain_vec):
    return (
        values
        * lax.rsqrt(jnp.mean(values * values, axis=-1, keepdims=True) + epsilon)
        * gain_vec.astype(jnp.float32)
    )


def rotate(values, position):
    half_dim = values.shape[-1] // 2
    frequency = rope_base ** (-(jnp.arange(half_dim, dtype=jnp.float32) * 2.0 / values.shape[-1]))
    angles = position.astype(jnp.float32)[:, None] * frequency[None, :]
    target_shape = (angles.shape[0],) + (1,) * (values.ndim - 2) + (half_dim,)
    cosine = jnp.cos(angles).reshape(target_shape)
    sine = jnp.sin(angles).reshape(target_shape)
    lower_half = values[..., :half_dim]
    upper_half = values[..., half_dim:]
    return jnp.concatenate(
        [lower_half * cosine - upper_half * sine, upper_half * cosine + lower_half * sine], axis=-1
    )


def attend(
    hidden_in, gain_in, w_query, w_key, w_value, query_gain, key_gain, cache_key, cache_val, lengths
):
    row_count = hidden_in.shape[0]
    kv_heads = w_key.shape[1] // HD
    head_group = w_query.shape[1] // w_key.shape[1]
    normed = rms_norm(hidden_in.astype(jnp.float32), gain_in).astype(jnp.bfloat16)
    query = jnp.dot(normed, w_query, preferred_element_type=jnp.float32).reshape(
        row_count, kv_heads, head_group, HD
    )
    key_raw = jnp.dot(normed, w_key, preferred_element_type=jnp.float32).reshape(
        row_count, kv_heads, HD
    )
    new_value = (
        jnp.dot(normed, w_value, preferred_element_type=jnp.float32)
        .astype(jnp.bfloat16)
        .reshape(row_count, kv_heads, HD)
    )
    query_rot = rotate(rms_norm(query, query_gain), lengths).astype(jnp.bfloat16)
    new_key = rotate(rms_norm(key_raw, key_gain), lengths).astype(jnp.bfloat16)
    score_scale = HD ** (-0.5)
    cache_score = (
        jnp.einsum("rkgd,rkjd->rkgj", query_rot, cache_key, preferred_element_type=jnp.float32)
        * score_scale
    )
    own_score = (
        jnp.einsum("rkgd,rkd->rkg", query_rot, new_key, preferred_element_type=jnp.float32)
        * score_scale
    )
    in_cache = jnp.arange(cache_key.shape[2])[None, None, None, :] < lengths[:, None, None, None]
    masked = jnp.where(in_cache, cache_score, -1e30)
    row_max = jnp.maximum(jnp.max(masked, axis=-1), own_score)
    cache_exp = jnp.where(in_cache, jnp.exp(masked - row_max[..., None]), 0.0)
    own_exp = jnp.exp(own_score - row_max)
    denom_sum = jnp.sum(cache_exp, axis=-1) + own_exp
    cache_prob = (cache_exp / denom_sum[..., None]).astype(jnp.bfloat16)
    own_prob = (own_exp / denom_sum).astype(jnp.bfloat16)
    attended = jnp.einsum(
        "rkgj,rkjd->rkgd", cache_prob, cache_val, preferred_element_type=jnp.float32
    )
    attended = (
        attended
        + own_prob.astype(jnp.float32)[..., None] * new_value.astype(jnp.float32)[:, :, None, :]
    )
    attended = attended.astype(jnp.bfloat16).reshape(row_count, kv_heads * head_group * HD)
    return (attended, new_key, new_value)


def body(
    state,
    gain_in,
    w_query,
    w_key,
    w_value,
    w_output,
    query_gain,
    key_gain,
    cache_keys,
    cache_values,
    lengths,
):
    hidden_in = state[0]
    projection = w_output[0]
    attended, new_key, new_value = attend(
        hidden_in,
        gain_in[0],
        w_query[0],
        w_key[0],
        w_value[0],
        query_gain[0],
        key_gain[0],
        cache_keys[0],
        cache_values[0],
        lengths[0],
    )
    partial_value = jnp.dot(attended, projection, preferred_element_type=jnp.float32)
    summed = lax.psum(partial_value, "tensor")
    result = (hidden_in.astype(jnp.float32) + summed).astype(jnp.bfloat16)
    handed = shifted(result, "section", 1)
    return (handed[None], new_key[None], new_value[None])


def solution(mesh):
    placed = (
        P("section", None, None),
        P("section", None),
        P("section", None, "tensor"),
        P("section", None, "tensor"),
        P("section", None, "tensor"),
        P("section", "tensor", None),
        P("section", None),
        P("section", None),
        P("section", None, "tensor", None, None),
        P("section", None, "tensor", None, None),
        P("section", None),
    )
    return jax.shard_map(
        body,
        mesh=mesh,
        in_specs=placed,
        out_specs=(
            P("section", None, None),
            P("section", None, "tensor", None),
            P("section", None, "tensor", None),
        ),
        check_vma=False,
    )
```

profile of v0, /device:TPU:1, one launch (start us, length us, event | category | flops | bytes accessed | tf_op | source)
XLA Modules:
  0.0 86.0 jit_solution(5686281708907500587)
XLA Ops:
  7.2 0.0 copy-start
  7.2 0.0 copy-start.3
  7.2 0.0 copy-start.4
  7.2 0.0 all-reduce.2.cloned.1.call-start
  7.2 0.0 copy-start.1
  7.3 0.8 bitcast_convert_fusion.2
  8.1 1.1 %bitcast_convert_fusion.1 = f32[128]{0:T(128)S(1)} fusion(bf16[1,128]{1,0:T(2,128)(2,1)} %param.17), kind=kLoop, calls=%fused_computation.67 | loop fusion | flops 128 | bytes 768 | tf_op jit(solution)/shard_map/convert_element_type | solution.py:23
  9.2 0.7 bitcast_convert_fusion
  9.8 1.0 %fusion.14 = f32[16]{0:T(128)S(1)} fusion(bf16[1,16,2560]{2,1,0:T(8,128)(2,1)} %param.11), kind=kLoop, calls=%fused_computation.17 | loop fusion | flops 122864 | bytes 81984 | tf_op jit(solution)/shard_map/reduce_sum | solution.py:22
  10.8 0.7 iota_compare_fusion
  11.6 0.7 convert_reduce_fusion
  12.3 1.5 %multiply_reduce_fusion.1 = (f32[16]{0:T(128)S(1)}, f32[16,128]{1,0:T(8,128)S(1)}) fusion(bf16[1,2560,128]{2,1,0:T(8,128)(2,1)} %param.14, bf16[1,16,2560]{2,1,0:T(8,128)(2,1)} %param.11, f32[2560]{0:T(1024)S(1)} %convert_reduce_fusion, f32[16]{0:T(128)S(1)} %add_rsqrt_fusion.2), kind=kOutput, calls=%fused_computation.56 | convolution fusion | flops 10653680 | bytes 755840 | tf_op jit(solution)/shard_map/dot_general | solution.py:51
  13.8 0.1 multiply_cosine_fusion.1
  14.0 0.1 multiply_bitcast_fusion
  14.0 0.1 fusion.35
  14.2 0.0 copy-done
  14.2 1.7 %fusion.48 = (f32[16,128]{1,0:T(8,128)S(1)}, bf16[16,128]{1,0:T(8,128)(2,1)}) fusion(bf16[1,2560,128]{2,1,0:T(8,128)(2,1)S(1)} %copy-done, bf16[1,16,2560]{2,1,0:T(8,128)(2,1)} %param.11, f32[2560]{0:T(1024)S(1)} %convert_reduce_fusion, f32[16]{0:T(128)S(1)} %add_rsqrt_fusion.2), kind=kOutput, calls=%fused_computation.75 | convolution fusion | flops 10653696 | bytes 759872 | tf_op jit(solution)/shard_map/dot_general | solution.py:55
  15.9 0.0 copy-start.2
  15.9 3.4 %fusion.4 = f32[2,8,8,128]{3,1,2,0:T(8,128)S(1)} fusion(bf16[1,2560,1024]{2,1,0:T(8,128)(2,1)} %param.13, bf16[1,16,2560]{2,1,0:T(8,128)(2,1)} %param.11, f32[2560]{0:T(1024)S(1)} %convert_reduce_fusion, f32[16]{0:T(128)S(1)} %add_rsqrt_fusion.2), kind=kOutput, calls=%fused_computation.4 | convolution fusion | flops 84049920 | bytes 5400640 | tf_op jit(solution)/shard_map/dot_general | solution.py:48
  19.3 0.1 multiply_reduce_fusion
  19.4 0.1 maximum_bitcast_fusion
  19.5 0.1 multiply_multiply_fusion
  19.6 0.1 fusion.22
  19.7 0.2 fusion.38
  19.9 0.0 copy-done.3
  19.9 0.3 fusion.49
  20.2 0.2 fusion.21
  20.5 0.0 copy-done.4
  20.5 0.2 fusion.8
  20.7 0.0 copy-done.1
  20.7 1.5 %fusion = f32[16,2560]{1,0:T(8,128)} fusion(bf16[1,1024,2560]{2,1,0:T(8,128)(2,1)S(1)} %copy-done.1, bf16[2,8,8,128]{3,2,1,0:T(8,128)(2,1)S(1)} %bitcast.85), kind=kOutput, calls=%fused_computation | convolution fusion | flops 83886080 | bytes 5439488 | tf_op jit(solution)/shard_map/dot_general | solution.py:116
  22.2 0.0 all-reduce.2.cloned.1.call-update
  22.2 45.4 %all-reduce.2.cloned.1.call-done = f32[16,2560]{1,0:T(8,128)} async-done(((f32[16,2560]{1,0:T(8,128)}), f32[16,2560]{1,0:T(8,128)}) %all-reduce.2.cloned.1.call-update) | async-done | bytes 163856 | tf_op jit(solution)/shard_map/psum | solution.py:117
  67.6 0.0 copy-done.2
  67.6 0.9 %fusion.15 = bf16[16,2560]{1,0:T(8,128)(2,1)S(1)} fusion(f32[16,2560]{1,0:T(8,128)} %all-reduce.2.cloned.1.call-done, bf16[1,16,2560]{2,1,0:T(8,128)(2,1)S(1)} %copy-done.2), kind=kLoop, calls=%fused_computation.18 | loop fusion | flops 122880 | bytes 327680 | tf_op jit(solution)/shard_map/convert_element_type | solution.py:118
  68.6 1.4 %collective-permute-start = (bf16[16,2560]{1,0:T(8,128)(2,1)S(1)}, bf16[16,2560]{1,0:T(8,128)(2,1)S(1)}, u32[]{:S(2)}, u32[]{:S(2)}) collective-permute-start(bf16[16,2560]{1,0:T(8,128)(2,1)S(1)} %fusion.15), channel_id=1, source_target_pairs={{0,4},{4,8},{8,12},{12,16},{16,20},{20,24},{24,28},{28,32},{32,36}... | collective-permute-start | bytes 245768 | tf_op jit(solution)/shard_map/ppermute | solution.py:16
  69.9 0.7 pad_maximum_fusion.3
  70.6 7.9 %collective-permute-done = bf16[16,2560]{1,0:T(8,128)(2,1)S(1)} collective-permute-done((bf16[16,2560]{1,0:T(8,128)(2,1)S(1)}, bf16[16,2560]{1,0:T(8,128)(2,1)S(1)}, u32[]{:S(2)}, u32[]{:S(2)}) %collective-permute-start) | collective-permute-done | bytes 81952 | tf_op jit(solution)/shard_map/ppermute | solution.py:16
  78.5 0.6 copy.26
  (7 shorter events, 0.1 us)
Async XLA Ops:
  7.2 7.0 %copy-start = (bf16[1,2560,128]{2,1,0:T(8,128)(2,1)S(1)}, bf16[1,2560,128]{2,1,0:T(8,128)(2,1)}, u32[]{:S(2)}) copy-start(bf16[1,2560,128]{2,1,0:T(8,128)(2,1)} %param.15) | copy-start | bytes 1966084
  7.2 12.7 %copy-start.3 = (bf16[1,16,1,32,128]{4,3,2,1,0:T(8,128)(2,1)S(1)}, bf16[1,16,1,32,128]{4,3,2,1,0:T(8,128)(2,1)}, u32[]{:S(2)}) copy-start(bf16[1,16,1,32,128]{4,3,2,1,0:T(8,128)(2,1)} %param.19) | copy-start | bytes 393220
  7.2 13.3 %copy-start.4 = (bf16[1,16,1,32,128]{4,3,2,1,0:T(8,128)(2,1)S(1)}, bf16[1,16,1,32,128]{4,3,2,1,0:T(8,128)(2,1)}, u32[]{:S(2)}) copy-start(bf16[1,16,1,32,128]{4,3,2,1,0:T(8,128)(2,1)} %param.20) | copy-start | bytes 393220
  7.2 60.4 %all-reduce.2.cloned.1.call-start = ((), (), s32[]{:S(2)}) async-start(), calls=%async_computation | async-start | bytes 327680 | tf_op jit(solution)/shard_map/psum | solution.py:117
  7.2 13.5 %copy-start.1 = (bf16[1,1024,2560]{2,1,0:T(8,128)(2,1)S(1)}, bf16[1,1024,2560]{2,1,0:T(8,128)(2,1)}, u32[]{:S(2)}) copy-start(bf16[1,1024,2560]{2,1,0:T(8,128)(2,1)} %param.16) | copy-start | bytes 15728644
  15.9 51.7 %copy-start.2 = (bf16[1,16,2560]{2,1,0:T(8,128)(2,1)S(1)}, bf16[1,16,2560]{2,1,0:T(8,128)(2,1)}, u32[]{:S(2)}) copy-start(bf16[1,16,2560]{2,1,0:T(8,128)(2,1)} %param.11) | copy-start | bytes 245764
  68.6 10.0 %collective-permute-start = (bf16[16,2560]{1,0:T(8,128)(2,1)S(1)}, bf16[16,2560]{1,0:T(8,128)(2,1)S(1)}, u32[]{:S(2)}, u32[]{:S(2)}) collective-permute-start(bf16[16,2560]{1,0:T(8,128)(2,1)S(1)} %fusion.15), channel_id=1, source_target_pairs={{0,4},{4,8},{8,12},{12,16},{16,20},{20,24},{24,28},{28,32},{32,36}... | collective-permute-start | bytes 245768 | tf_op jit(solution)/shard_map/ppermute | solution.py:16
Sparse Core Ops, SparseCore 0:
  22.3 45.2 all-reduce.1
where the time goes:
time: 86.3 us; the launch traced here: 86 us
  waiting for transfers between devices  53.4 us (62%)
  between operations  14.2 us (16%)
  matrix products  8.84 us (10%)
  other arithmetic  7.52 us (9%)
  starting transfers between devices  1.39 us (2%)
    psum x1, waiting for transfers between devices, body(): summed = lax.psum(partial_value, 'tensor')  45.4 us
    ppermute x1, waiting for transfers between devices, shifted(): return lax.ppermute(value, axis, pairs)  7.94 us
    dot_general x1, matrix products, attend(): jnp.dot(normed, w_query, preferred_element_type=jnp.float32)  3.39 us
    dot_general x1, matrix products, attend(): jnp.dot(normed, w_value, preferred_element_type=jnp.float32)  1.75 us
    convert_element_type x2, other arithmetic, rms_norm(): gain_vec.astype(jnp.float32)  1.73 us
  transfers between devices with their start and end apart: 2, of which 2 were waited for; matrix products, arithmetic and copies ran while one was open for 1% of the time, Pallas kernels for 0%

commit v1 on v0

v1 whole, which is shorter than its diff:
```python
import functools

import jax
import jax.numpy as jnp
from jax import lax
from jax.experimental import pallas as pl
from jax.experimental.pallas import tpu as pltpu
from jax.sharding import PartitionSpec as P

HD = 128
EPSILON = 1e-06
LOG_BASE = 13.815510557964274
NEG = -1e30
F32 = jnp.float32
BF16 = jnp.bfloat16


def dot(a, b):
    return jnp.dot(a, b, preferred_element_type=F32)


def kernel(
    state, gain, wq, wk, wv, wo, qgain, kgain, ckey, cval, lens,
    part, newk, newv,
    state_v, gain_v, wq_v, wkv_v, wo_v, qgain_v, kgain_v, key_v, val_v, lens_v,
    sem, wq_sem, wo_sem,
):
    rows, width = state_v.shape[1:]
    slots = ckey.shape[1]
    cached = rows * slots
    group = wq.shape[2] // HD
    wq_parts, wo_parts = wq_sem.shape[0], wo_sem.shape[0]
    wq_rows, wo_rows = wq.shape[1] // wq_parts, wo.shape[1] // wo_parts

    def copy(src, dst, s):
        c = pltpu.make_async_copy(src, dst, s)
        c.start()
        return c

    c_state = copy(state, state_v, sem.at[0])
    c_gain = copy(gain, gain_v, sem.at[1])
    c_lens = copy(lens, lens_v, sem.at[2])
    c_qgain = copy(qgain, qgain_v, sem.at[3])
    c_kgain = copy(kgain, kgain_v, sem.at[4])
    c_wk = copy(wk.at[0], wkv_v.at[:, pl.ds(0, HD)], sem.at[5])
    c_wv = copy(wv.at[0], wkv_v.at[:, pl.ds(HD, HD)], sem.at[6])
    c_wq = [
        copy(wq.at[0, pl.ds(i * wq_rows, wq_rows)], wq_v.at[pl.ds(i * wq_rows, wq_rows)], wq_sem.at[i])
        for i in range(wq_parts)
    ]
    c_key = copy(ckey, key_v, sem.at[7])
    c_val = copy(cval, val_v, sem.at[8])
    c_wo = [
        copy(wo.at[0, pl.ds(i * wo_rows, wo_rows)], wo_v.at[pl.ds(i * wo_rows, wo_rows)], wo_sem.at[i])
        for i in range(wo_parts)
    ]

    c_lens.wait()
    row_i = lax.broadcasted_iota(jnp.int32, (rows, rows), 0)
    row_j = lax.broadcasted_iota(jnp.int32, (rows, rows), 1)
    length = jnp.sum(
        jnp.where(row_i == row_j, lens_v[...].astype(F32), 0.0), axis=1, keepdims=True
    )
    lane = lax.broadcasted_iota(jnp.int32, (rows, HD), 1)
    half = lax.rem(lane, HD // 2).astype(F32)
    angle = length * jnp.exp(half * (-2.0 * LOG_BASE / HD))
    cosine = jnp.cos(angle)
    sine = jnp.sin(angle)
    sine = jnp.where(lane < HD // 2, -sine, sine)

    c_state.wait()
    c_gain.wait()
    hidden = state_v[0].astype(F32)
    mean = jnp.mean(hidden * hidden, axis=-1, keepdims=True)
    normed = (hidden * lax.rsqrt(mean + EPSILON) * gain_v[...].astype(F32)).astype(BF16)

    def head_norm(x, gain_row):
        mean = jnp.mean(x * x, axis=-1, keepdims=True)
        x = x * lax.rsqrt(mean + EPSILON) * gain_row
        return (x * cosine + pltpu.roll(x, HD // 2, 1) * sine).astype(BF16)

    c_wk.wait()
    c_wv.wait()
    c_kgain.wait()
    key_value = dot(normed, wkv_v[...])
    new_key = head_norm(key_value[:, :HD], kgain_v[...].astype(F32))
    new_value = key_value[:, HD:].astype(BF16)
    newk[...] = new_key
    newv[...] = new_value

    query = jnp.zeros((rows, group * HD), F32)
    for i in range(wq_parts):
        c_wq[i].wait()
        at = i * wq_rows
        query = query + dot(normed[:, at : at + wq_rows], wq_v[at : at + wq_rows])
    c_qgain.wait()
    qgain_row = qgain_v[...].astype(F32)
    query_rot = jnp.concatenate(
        [head_norm(query[:, g * HD : (g + 1) * HD], qgain_row) for g in range(group)], axis=0
    )

    count = group * rows
    c_key.wait()
    last = (((1,), (1,)), ((), ()))
    pad = jnp.zeros((HD - rows, HD), BF16)
    keys = jnp.concatenate([key_v[...].reshape(cached, HD), new_key, pad], axis=0)
    scores = lax.dot_general(query_rot, keys, last, preferred_element_type=F32) * HD**-0.5
    spread = cached + HD
    at_row = lax.broadcasted_iota(jnp.int32, (rows, spread), 0)
    at_col = lax.broadcasted_iota(jnp.int32, (rows, spread), 1)
    slot = at_col - at_row * slots
    length_i = length.astype(jnp.int32)
    valid = ((slot >= 0) & (slot < length_i) & (at_col < cached)) | (at_col == cached + at_row)
    valid = jnp.where(valid, 1.0, 0.0)
    valid = jnp.concatenate([valid] * group, axis=0) > 0.5
    masked = jnp.where(valid, scores, NEG)
    top = jnp.max(masked, axis=-1, keepdims=True)
    weight = jnp.exp(masked - top)
    total = jnp.sum(weight, axis=-1, keepdims=True)
    probs = (weight * (1.0 / total)).astype(BF16)
    c_val.wait()
    values = jnp.concatenate([val_v[...].reshape(cached, HD), new_value, pad], axis=0)
    attended = dot(probs, values).astype(BF16)
    attended = jnp.concatenate([attended[g * rows : (g + 1) * rows] for g in range(group)], axis=1)

    first = lax.axis_index("tensor") == 0
    out = jnp.where(first, hidden, 0.0)
    for i in range(wo_parts):
        c_wo[i].wait()
        at = i * wo_rows
        out = out + dot(attended[:, at : at + wo_rows], wo_v[at : at + wo_rows])
    part[...] = out.astype(BF16)


def section_partial(args):
    state, gain, wq, wk, wv, wo, qgain, kgain, ckey, cval, lens = args
    rows, width = state.shape[1:]
    wq_parts, wo_parts = 10, 4
    any_space = pl.BlockSpec(memory_space=pltpu.HBM)
    vmem = pl.BlockSpec(memory_space=pltpu.VMEM)
    slots = ckey.shape[3]
    ckey = ckey.reshape(rows, slots, HD)
    cval = cval.reshape(rows, slots, HD)
    args = (state, gain, wq, wk, wv, wo, qgain, kgain, ckey, cval, lens)
    return pl.pallas_call(
        kernel,
        out_shape=(
            jax.ShapeDtypeStruct((rows, width), BF16),
            jax.ShapeDtypeStruct((rows, HD), BF16),
            jax.ShapeDtypeStruct((rows, HD), BF16),
        ),
        in_specs=[any_space] * len(args),
        out_specs=(vmem, vmem, vmem),
        scratch_shapes=[
            pltpu.VMEM(state.shape, BF16),
            pltpu.VMEM(gain.shape, BF16),
            pltpu.VMEM(wq.shape[1:], BF16),
            pltpu.VMEM((width, 2 * HD), BF16),
            pltpu.VMEM(wo.shape[1:], BF16),
            pltpu.VMEM(qgain.shape, BF16),
            pltpu.VMEM(kgain.shape, BF16),
            pltpu.VMEM(ckey.shape, BF16),
            pltpu.VMEM(cval.shape, BF16),
            pltpu.VMEM(lens.shape, jnp.int32),
            pltpu.SemaphoreType.DMA((9,)),
            pltpu.SemaphoreType.DMA((wq_parts,)),
            pltpu.SemaphoreType.DMA((wo_parts,)),
        ],
        compiler_params=pltpu.CompilerParams(vmem_limit_bytes=60 * 2**20),
        cost_estimate=pl.CostEstimate(
            flops=2 * rows * (wq.size + wk.size + wv.size + wo.size),
            bytes_accessed=2 * (wq.size + wk.size + wv.size + wo.size + ckey.size + cval.size),
            transcendentals=0,
        ),
    )(*args)


def body(sections, tensors, *args):
    def moved(x, step, flip):
        pairs = [
            (s * tensors + t, (s + step) % sections * tensors + (t ^ flip))
            for s in range(sections)
            for t in range(tensors)
        ]
        return lax.ppermute(x, ("section", "tensor"), pairs)

    part, new_key, new_value = section_partial(args)
    pair = (part.astype(F32) + moved(part, 0, 1).astype(F32)).astype(BF16)
    near, far = moved(pair, 1, 0), moved(pair, 1, 2)
    handed = (near.astype(F32) + far.astype(F32)).astype(BF16)
    rows = part.shape[0]
    return handed[None], new_key.reshape(1, rows, 1, HD), new_value.reshape(1, rows, 1, HD)


def solution(mesh):
    placed = (
        P("section", None, None),
        P("section", None),
        P("section", None, "tensor"),
        P("section", None, "tensor"),
        P("section", None, "tensor"),
        P("section", "tensor", None),
        P("section", None),
        P("section", None),
        P("section", None, "tensor", None, None),
        P("section", None, "tensor", None, None),
        P("section", None),
    )
    return jax.shard_map(
        functools.partial(body, mesh.shape["section"], mesh.shape["tensor"]),
        mesh=mesh,
        in_specs=placed,
        out_specs=(
            P("section", None, None),
            P("section", None, "tensor", None),
            P("section", None, "tensor", None),
        ),
        check_vma=False,
    )
```

time: 86.3 us -> 27.8 us (0.32)
  waiting for transfers between devices: 53.4 us -> 11.5 us
  between operations: 14.2 us -> 0.65 us
  matrix products: 8.84 us -> 0 us
  Pallas kernels: 0 us -> 8.03 us
  other arithmetic: 7.52 us -> 1.57 us
  starting transfers between devices: 1.39 us -> 5.96 us
    psum x1 -> x0, waiting for transfers between devices: 45.4 us -> none  [body(): summed = lax.psum(partial_value, 'tensor')]
    dot_general x7 -> x0, matrix products: 8.84 us -> none  [the longest x1 3.39 us: attend(): jnp.dot(normed, w_query, preferred_element_type=jnp.float32)]
    pallas_call x0 -> x1, Pallas kernels: none -> 8.03 us  [section_partial(): pl.pallas_call(kernel, out_shape=(jax.ShapeDtypeStruct((rows, width), BF1...]
    ppermute x1 -> x3, starting transfers between devices: 1.35 us -> 5.96 us  [moved(): return lax.ppermute(x, ('section', 'tensor'), pairs)]
    ppermute x1 -> x3, waiting for transfers between devices: 7.94 us -> 11.5 us  [moved(): return lax.ppermute(x, ('section', 'tensor'), pairs)]
    convert_element_type x4 -> x1, other arithmetic: 3.47 us -> 0.91 us  [body(): pair = (part.astype(F32) + moved(part, 0, 1).astype(F32)).astype(BF16)]
    reduce_sum x3 -> x0, other arithmetic: 1.29 us -> none  [the longest x2 1.11 us: rms_norm(): jnp.mean(values * values, axis=-1, keepdims=True) + epsilon]
    mul x3 -> x0, other arithmetic: 0.88 us -> none  [rms_norm(): values * lax.rsqrt(jnp.mean(values * values, axis=-1, keepdims=True) + ep...]
  transfers between devices with their start and end apart: 2 -> 3, of which waited for: 2 -> 3; matrix products, arithmetic and copies ran while one was open for 1% -> 0% of each run, Pallas kernels for 0% -> 0%
where the time goes in v1:
time: 27.8 us; the launch traced here: 27.7 us
  waiting for transfers between devices  11.5 us (41%)
  Pallas kernels  8.03 us (29%)
  starting transfers between devices  5.96 us (21%)
  other arithmetic  1.57 us (6%)
  between operations  0.65 us (2%)
    ppermute x3, waiting for transfers between devices, moved(): return lax.ppermute(x, ('section', 'tensor'), pairs)  11.5 us
    pallas_call x1, Pallas kernels, section_partial(): pl.pallas_call(kernel, out_shape=(jax.ShapeDtypeStruct((rows, width), BF1...  8.03 us
    ppermute x3, starting transfers between devices, moved(): return lax.ppermute(x, ('section', 'tensor'), pairs)  5.96 us
    convert_element_type x1, other arithmetic, body(): pair = (part.astype(F32) + moved(part, 0, 1).astype(F32)).astype(BF16)  0.91 us
    broadcast_in_dim x1, other arithmetic, body(): handed[None]  0.66 us
  transfers between devices with their start and end apart: 3, of which 3 were waited for; matrix products, arithmetic and copies ran while one was open for 0% of the time, Pallas kernels for 0%

profile of v1, /device:TPU:1, one launch (start us, length us, event | category | flops | bytes accessed | tf_op | source)
XLA Modules:
  0.0 27.7 jit_solution(14624579740045532893)
XLA Ops:
  0.6 8.0 %shard_map.130 = (bf16[16,2560]{1,0:T(8,128)(2,1)}, bf16[16,128]{1,0:T(8,128)(2,1)}, bf16[16,128]{1,0:T(8,128)(2,1)}) custom-call(bf16[1,16,2560]{2,1,0:T(8,128)(2,1)} %state.1, bf16[1,2560]{1,0:T(2,128)(2,1)} %gain.1, bf16[1,2560,1024]{2,1,0:T(8,128)(2,1)} %wq.1, bf16[1,2560,128]{2,1,0:T(8,128)(2,1)} %wk.1, bf16[1,2560,128]{2,1,0:T(8,128)(2,1)} %wv.1, ...), custom_call_target="tpu_custom_call" | custom-call | flops 188743680 | bytes 12058624 | tf_op jit(solution)/shard_map/pallas_call | solution.py:145
  8.7 3.3 %collective-permute-start = (bf16[16,2560]{1,0:T(8,128)(2,1)}, bf16[16,2560]{1,0:T(8,128)(2,1)S(1)}, u32[]{:S(2)}, u32[]{:S(2)}) collective-permute-start(bf16[16,2560]{1,0:T(8,128)(2,1)} %get-tuple-element.6), channel_id=1, source_target_pairs={{0,1},{1,0},{2,3},{3,2},{4,5},{5,4},{6,7},{7,6},{8,9},{9,8},{10,11... | collective-permute-start | bytes 245768 | tf_op jit(solution)/shard_map/ppermute | solution.py:185
  12.0 1.1 %collective-permute-done = bf16[16,2560]{1,0:T(8,128)(2,1)S(1)} collective-permute-done((bf16[16,2560]{1,0:T(8,128)(2,1)}, bf16[16,2560]{1,0:T(8,128)(2,1)S(1)}, u32[]{:S(2)}, u32[]{:S(2)}) %collective-permute-start) | collective-permute-done | bytes 81952 | tf_op jit(solution)/shard_map/ppermute | solution.py:185
  13.1 0.9 %add_convert_fusion.1 = bf16[16,2560]{1,0:T(8,128)(2,1)S(1)} fusion(bf16[16,2560]{1,0:T(8,128)(2,1)S(1)} %collective-permute-done, bf16[16,2560]{1,0:T(8,128)(2,1)} %get-tuple-element.6), kind=kLoop, calls=%fused_computation.1 | loop fusion | flops 163840 | bytes 245760 | tf_op jit(solution)/shard_map/convert_element_type | solution.py:188
  14.0 1.0 %collective-permute-start.2 = (bf16[16,2560]{1,0:T(8,128)(2,1)S(1)}, bf16[16,2560]{1,0:T(8,128)(2,1)S(1)}, u32[]{:S(2)}, u32[]{:S(2)}) collective-permute-start(bf16[16,2560]{1,0:T(8,128)(2,1)S(1)} %add_convert_fusion.1), channel_id=1, source_target_pairs={{0,6},{1,7},{2,4},{3,5},{4,10},{5,11},{6,8},{7,9},{8,14},{9,15},{1... | collective-permute-start | bytes 245768 | tf_op jit(solution)/shard_map/ppermute | solution.py:185
  15.0 1.6 %collective-permute-start.1 = (bf16[16,2560]{1,0:T(8,128)(2,1)S(1)}, bf16[16,2560]{1,0:T(8,128)(2,1)S(1)}, u32[]{:S(2)}, u32[]{:S(2)}) collective-permute-start(bf16[16,2560]{1,0:T(8,128)(2,1)S(1)} %add_convert_fusion.1), channel_id=1, source_target_pairs={{0,4},{1,5},{2,6},{3,7},{4,8},{5,9},{6,10},{7,11},{8,12},{9,13},{1... | collective-permute-start | bytes 245768 | tf_op jit(solution)/shard_map/ppermute | solution.py:185
  16.7 8.5 %collective-permute-done.2 = bf16[16,2560]{1,0:T(8,128)(2,1)S(1)} collective-permute-done((bf16[16,2560]{1,0:T(8,128)(2,1)S(1)}, bf16[16,2560]{1,0:T(8,128)(2,1)S(1)}, u32[]{:S(2)}, u32[]{:S(2)}) %collective-permute-start.2) | collective-permute-done | bytes 81952 | tf_op jit(solution)/shard_map/ppermute | solution.py:185
  25.1 1.9 %collective-permute-done.1 = bf16[16,2560]{1,0:T(8,128)(2,1)S(1)} collective-permute-done((bf16[16,2560]{1,0:T(8,128)(2,1)S(1)}, bf16[16,2560]{1,0:T(8,128)(2,1)S(1)}, u32[]{:S(2)}, u32[]{:S(2)}) %collective-permute-start.1) | collective-permute-done | bytes 81952 | tf_op jit(solution)/shard_map/ppermute | solution.py:185
  27.1 0.7 %fusion = bf16[1,16,2560]{2,1,0:T(8,128)(2,1)} fusion(bf16[16,2560]{1,0:T(8,128)(2,1)S(1)} %collective-permute-done.2, bf16[16,2560]{1,0:T(8,128)(2,1)S(1)} %collective-permute-done.1), kind=kLoop, calls=%fused_computation.2 | loop fusion | flops 163840 | bytes 245760 | tf_op jit(solution)/shard_map/broadcast_in_dim | solution.py:192
Async XLA Ops:
  8.7 4.5 %collective-permute-start = (bf16[16,2560]{1,0:T(8,128)(2,1)}, bf16[16,2560]{1,0:T(8,128)(2,1)S(1)}, u32[]{:S(2)}, u32[]{:S(2)}) collective-permute-start(bf16[16,2560]{1,0:T(8,128)(2,1)} %get-tuple-element.6), channel_id=1, source_target_pairs={{0,1},{1,0},{2,3},{3,2},{4,5},{5,4},{6,7},{7,6},{8,9},{9,8},{10,11... | collective-permute-start | bytes 245768 | tf_op jit(solution)/shard_map/ppermute | solution.py:185
  14.0 11.1 %collective-permute-start.2 = (bf16[16,2560]{1,0:T(8,128)(2,1)S(1)}, bf16[16,2560]{1,0:T(8,128)(2,1)S(1)}, u32[]{:S(2)}, u32[]{:S(2)}) collective-permute-start(bf16[16,2560]{1,0:T(8,128)(2,1)S(1)} %add_convert_fusion.1), channel_id=1, source_target_pairs={{0,6},{1,7},{2,4},{3,5},{4,10},{5,11},{6,8},{7,9},{8,14},{9,15},{1... | collective-permute-start | bytes 245768 | tf_op jit(solution)/shard_map/ppermute | solution.py:185
  15.0 12.0 %collective-permute-start.1 = (bf16[16,2560]{1,0:T(8,128)(2,1)S(1)}, bf16[16,2560]{1,0:T(8,128)(2,1)S(1)}, u32[]{:S(2)}, u32[]{:S(2)}) collective-permute-start(bf16[16,2560]{1,0:T(8,128)(2,1)S(1)} %add_convert_fusion.1), channel_id=1, source_target_pairs={{0,4},{1,5},{2,6},{3,7},{4,8},{5,9},{6,10},{7,11},{8,12},{9,13},{1... | collective-permute-start | bytes 245768 | tf_op jit(solution)/shard_map/ppermute | solution.py:185

commit v2 on v1

v2 whole, which is shorter than its diff:
```python
import functools

import jax
import jax.numpy as jnp
from jax import lax
from jax.experimental import pallas as pl
from jax.experimental.pallas import tpu as pltpu
from jax.sharding import PartitionSpec as P

HD = 128
EPSILON = 1e-06
BLOCKS = 2
LOG_BASE = 13.815510557964274
NEG = -1e30
F32 = jnp.float32
BF16 = jnp.bfloat16


def dot(a, b):
    return jnp.dot(a, b, preferred_element_type=F32)


def kernel(
    state, gain, wq, wk, wv, wo, qgain, kgain, ckey, cval, lens,
    part, newk, newv,
    state_v, gain_v, wq_v, wkv_v, wo_v, qgain_v, kgain_v, key_v, val_v, lens_v, newk_v, newv_v,
    sem, wq_sem, wo_sem,
):
    rows, width = state_v.shape[1:]
    slots = ckey.shape[1]
    cached = rows * slots
    heads = wq.shape[2] // HD
    blocks = wq_sem.shape[0]
    group = heads // blocks
    span = group * HD
    last = (((1,), (1,)), ((), ()))

    def copy(src, dst, s):
        c = pltpu.make_async_copy(src, dst, s)
        c.start()
        return c

    c_state = copy(state, state_v, sem.at[0])
    c_gain = copy(gain, gain_v, sem.at[1])
    c_lens = copy(lens, lens_v, sem.at[2])
    c_qgain = copy(qgain, qgain_v, sem.at[3])
    c_kgain = copy(kgain, kgain_v, sem.at[4])
    c_wk = copy(wk.at[0], wkv_v.at[:, pl.ds(0, HD)], sem.at[5])
    c_wv = copy(wv.at[0], wkv_v.at[:, pl.ds(HD, HD)], sem.at[6])
    c_key = copy(ckey, key_v, sem.at[7])
    c_val = copy(cval, val_v, sem.at[8])
    c_wq = [copy(wq.at[0, :, pl.ds(i * span, span)], wq_v.at[i], wq_sem.at[i]) for i in range(blocks)]
    c_wo = []

    def start_wo():
        i = len(c_wo)
        at = pl.ds(i * span, span)
        c_wo.append(copy(wo.at[0, at], wo_v.at[at], wo_sem.at[i]))

    c_lens.wait()
    c_state.wait()
    c_gain.wait()
    c_qgain.wait()
    c_kgain.wait()
    row_i = lax.broadcasted_iota(jnp.int32, (rows, rows), 0)
    row_j = lax.broadcasted_iota(jnp.int32, (rows, rows), 1)
    length = jnp.sum(
        jnp.where(row_i == row_j, lens_v[...].astype(F32), 0.0), axis=1, keepdims=True
    )
    lane = lax.broadcasted_iota(jnp.int32, (rows, HD), 1)
    half = lax.rem(lane, HD // 2).astype(F32)
    angle = length * jnp.exp(half * (-2.0 * LOG_BASE / HD))
    cosine = jnp.cos(angle)
    sine = jnp.sin(angle)
    sine = jnp.where(lane < HD // 2, -sine, sine)
    spread = cached + HD
    at_row = lax.broadcasted_iota(jnp.int32, (rows, spread), 0)
    at_col = lax.broadcasted_iota(jnp.int32, (rows, spread), 1)
    slot = at_col - at_row * slots
    valid = (slot >= 0) & (slot < length.astype(jnp.int32)) & (at_col < cached)
    valid = valid | (at_col == cached + at_row)
    bias = jnp.where(valid, 0.0, NEG)

    hidden = state_v[0].astype(F32)
    mean = jnp.mean(hidden * hidden, axis=-1, keepdims=True)
    normed = (hidden * lax.rsqrt(mean + EPSILON) * gain_v[...].astype(F32)).astype(BF16)
    qgain_row = qgain_v[...].astype(F32)

    def head_norm(x, gain_row):
        mean = jnp.mean(x * x, axis=-1, keepdims=True)
        x = x * lax.rsqrt(mean + EPSILON) * gain_row
        return (x * cosine + pltpu.roll(x, HD // 2, 1) * sine).astype(BF16)

    c_wk.wait()
    c_wv.wait()
    key_value = dot(normed, wkv_v[...])
    new_key = head_norm(key_value[:, :HD], kgain_v[...].astype(F32))
    new_value = key_value[:, HD:].astype(BF16)
    newk_v[...] = new_key
    newv_v[...] = new_value
    c_newk = copy(newk_v, newk, sem.at[9])
    c_newv = copy(newv_v, newv, sem.at[10])
    pad = jnp.zeros((HD - rows, HD), BF16)

    def attend(query):
        query_rot = jnp.concatenate(
            [head_norm(query[:, g * HD : (g + 1) * HD], qgain_row) for g in range(group)], axis=0
        )
        keys = jnp.concatenate([key_v[...].reshape(cached, HD), new_key, pad], axis=0)
        scores = lax.dot_general(query_rot, keys, last, preferred_element_type=F32) * HD**-0.5
        masked = (scores.reshape(group, rows, spread) + bias).reshape(group * rows, spread)
        top = jnp.max(masked, axis=-1, keepdims=True)
        weight = jnp.exp(masked - top)
        total = jnp.sum(weight, axis=-1, keepdims=True)
        probs = (weight * (1.0 / total)).astype(BF16)
        values = jnp.concatenate([val_v[...].reshape(cached, HD), new_value, pad], axis=0)
        out = dot(probs, values).astype(BF16)
        return jnp.concatenate([out[g * rows : (g + 1) * rows] for g in range(group)], axis=1)

    first = lax.axis_index("tensor") == 0
    out = jnp.where(first, hidden, 0.0)
    c_wq[0].wait()
    start_wo()
    c_key.wait()
    c_val.wait()
    query = dot(normed, wq_v[0])
    attended = []
    for i in range(1, blocks):
        c_wq[i].wait()
        start_wo()
        following = dot(normed, wq_v[i])
        attended.append(attend(query))
        query = following
    for i in range(blocks):
        c_wo[i].wait()
        if i == 0:
            attended.append(attend(query))
        out = out + dot(attended[i], wo_v[i * span : (i + 1) * span])
    part[...] = out.astype(BF16)
    c_newk.wait()
    c_newv.wait()


def section_partial(args):
    state, gain, wq, wk, wv, wo, qgain, kgain, ckey, cval, lens = args
    rows, width = state.shape[1:]
    any_space = pl.BlockSpec(memory_space=pltpu.HBM)
    vmem = pl.BlockSpec(memory_space=pltpu.VMEM)
    slots = ckey.shape[3]
    ckey = ckey.reshape(rows, slots, HD)
    cval = cval.reshape(rows, slots, HD)
    args = (state, gain, wq, wk, wv, wo, qgain, kgain, ckey, cval, lens)
    args = [pltpu.with_memory_space_constraint(a, pltpu.HBM) for a in args]
    return pl.pallas_call(
        kernel,
        out_shape=(
            pltpu.VMEM((rows, width), BF16),
            pltpu.HBM((rows, HD), BF16),
            pltpu.HBM((rows, HD), BF16),
        ),
        in_specs=[any_space] * len(args),
        out_specs=(vmem, any_space, any_space),
        scratch_shapes=[
            pltpu.VMEM(state.shape, BF16),
            pltpu.VMEM(gain.shape, BF16),
            pltpu.VMEM((BLOCKS, width, wq.shape[2] // BLOCKS), BF16),
            pltpu.VMEM((width, 2 * HD), BF16),
            pltpu.VMEM(wo.shape[1:], BF16),
            pltpu.VMEM(qgain.shape, BF16),
            pltpu.VMEM(kgain.shape, BF16),
            pltpu.VMEM(ckey.shape, BF16),
            pltpu.VMEM(cval.shape, BF16),
            pltpu.VMEM(lens.shape, jnp.int32),
            pltpu.VMEM((rows, HD), BF16),
            pltpu.VMEM((rows, HD), BF16),
            pltpu.SemaphoreType.DMA((11,)),
            pltpu.SemaphoreType.DMA((BLOCKS,)),
            pltpu.SemaphoreType.DMA((BLOCKS,)),
        ],
        compiler_params=pltpu.CompilerParams(vmem_limit_bytes=24 * 2**20),
        cost_estimate=pl.CostEstimate(
            flops=2 * rows * (wq.size + wk.size + wv.size + wo.size),
            bytes_accessed=2 * (wq.size + wk.size + wv.size + wo.size + ckey.size + cval.size),
            transcendentals=0,
        ),
    )(*args)


ROUTES = (
    ((0, 2), (1, 1), (0, 0), (1, 3)),
    ((0, 2), (1, 3), (0, 0), (1, 1)),
    ((0, 1), (1, 0), (0, 3), (1, 2)),
    ((0, 1), (1, 2), (0, 3), (1, 0)),
)
SWAP = ((0, 1), (0, 0), (0, 3), (0, 2))


def added(a, b):
    return (a.astype(F32) + b.astype(F32)).astype(BF16)


def body(sections, *args):
    def moved(x, route):
        pairs = [
            (s * len(route) + t, (s + step) % sections * len(route) + to)
            for s in range(sections)
            for t, (step, to) in enumerate(route)
        ]
        return lax.ppermute(x, ("section", "tensor"), pairs)

    part, new_key, new_value = section_partial(args)
    pair = added(part, moved(part, SWAP))
    a, b, c, d = [moved(pair, route) for route in ROUTES]
    odd = lax.axis_index("tensor") % 2 == 1
    handed = jnp.where(odd, added(b, a), added(d, c))
    rows = part.shape[0]
    return handed[None], new_key.reshape(1, rows, 1, HD), new_value.reshape(1, rows, 1, HD)


def solution(mesh):
    placed = (
        P("section", None, None),
        P("section", None),
        P("section", None, "tensor"),
        P("section", None, "tensor"),
        P("section", None, "tensor"),
        P("section", "tensor", None),
        P("section", None),
        P("section", None),
        P("section", None, "tensor", None, None),
        P("section", None, "tensor", None, None),
        P("section", None),
    )
    return jax.shard_map(
        functools.partial(body, mesh.shape["section"]),
        mesh=mesh,
        in_specs=placed,
        out_specs=(
            P("section", None, None),
            P("section", None, "tensor", None),
            P("section", None, "tensor", None),
        ),
        check_vma=False,
    )
```

time: 27.8 us -> 22.9 us (0.82)
  waiting for transfers between devices: 11.5 us -> 7.83 us
  Pallas kernels: 8.03 us -> 5.69 us
  starting transfers between devices: 5.96 us -> 7.86 us
  other arithmetic: 1.57 us -> 0.7 us
    ppermute x3 -> x5, waiting for transfers between devices: 11.5 us -> 7.83 us  [moved(): return lax.ppermute(x, ('section', 'tensor'), pairs)]
    pallas_call x1, Pallas kernels: 8.03 us -> 5.69 us  [section_partial(): pl.pallas_call(kernel, out_shape=(pltpu.VMEM((rows, width), BF16), pltpu....]
    ppermute x3 -> x5, starting transfers between devices: 5.96 us -> 7.86 us  [moved(): return lax.ppermute(x, ('section', 'tensor'), pairs)]
    convert_element_type x1, other arithmetic: 0.91 us -> 0.02 us  [added(): return (a.astype(F32) + b.astype(F32)).astype(BF16)]
  transfers between devices with their start and end apart: 3 -> 5, of which waited for: 3 -> 3; matrix products, arithmetic and copies ran while one was open for 0% -> 0% of each run, Pallas kernels for 0% -> 0%
where the time goes in v2:
time: 22.9 us; the launch traced here: 22.7 us
  starting transfers between devices  7.86 us (34%)
  waiting for transfers between devices  7.83 us (34%)
  Pallas kernels  5.69 us (25%)
  other arithmetic  0.7 us (3%)
  between operations  0.66 us (3%)
    ppermute x5, starting transfers between devices, moved(): return lax.ppermute(x, ('section', 'tensor'), pairs)  7.86 us
    ppermute x5, waiting for transfers between devices, moved(): return lax.ppermute(x, ('section', 'tensor'), pairs)  7.83 us
    pallas_call x1, Pallas kernels, section_partial(): pl.pallas_call(kernel, out_shape=(pltpu.VMEM((rows, width), BF16), pltpu....  5.69 us
    broadcast_in_dim x1, other arithmetic, body(): handed[None]  0.68 us
  transfers between devices with their start and end apart: 5, of which 3 were waited for; matrix products, arithmetic and copies ran while one was open for 0% of the time, Pallas kernels for 0%

profile of v2, /device:TPU:1, one launch (start us, length us, event | category | flops | bytes accessed | tf_op | source)
XLA Modules:
  0.0 22.7 jit_solution(17744428692519125128)
XLA Ops:
  0.6 5.7 %shard_map.130 = (bf16[16,2560]{1,0:T(8,128)(2,1)S(1)}, bf16[16,128]{1,0:T(8,128)(2,1)}, bf16[16,128]{1,0:T(8,128)(2,1)}) custom-call(bf16[1,16,2560]{2,1,0:T(8,128)(2,1)} %state.1, bf16[1,2560]{1,0:T(2,128)(2,1)} %gain.1, bf16[1,2560,1024]{2,1,0:T(8,128)(2,1)} %wq.1, bf16[1,2560,128]{2,1,0:T(8,128)(2,1)} %wk.1, bf16[1,2560,128]{2,1,0:T(8,128)(2,1)} %wv.1, ...), custom_call_target="tpu_custom_call" | custom-call | flops 188743680 | bytes 12058624 | tf_op jit(solution)/shard_map/pallas_call | solution.py:154
  6.3 3.3 %collective-permute-start = (bf16[16,2560]{1,0:T(8,128)(2,1)S(1)}, bf16[16,2560]{1,0:T(8,128)(2,1)S(1)}, u32[]{:S(2)}, u32[]{:S(2)}) collective-permute-start(bf16[16,2560]{1,0:T(8,128)(2,1)S(1)} %get-tuple-element.6), channel_id=1, source_target_pairs={{0,1},{1,0},{2,3},{3,2},{4,5},{5,4},{6,7},{7,6},{8,9},{9,8},{10,11... | collective-permute-start | bytes 245768 | tf_op jit(solution)/shard_map/ppermute | solution.py:209
  9.7 0.9 %collective-permute-done = bf16[16,2560]{1,0:T(8,128)(2,1)S(1)} collective-permute-done((bf16[16,2560]{1,0:T(8,128)(2,1)S(1)}, bf16[16,2560]{1,0:T(8,128)(2,1)S(1)}, u32[]{:S(2)}, u32[]{:S(2)}) %collective-permute-start) | collective-permute-done | bytes 81952 | tf_op jit(solution)/shard_map/ppermute | solution.py:209
  10.6 0.1 collective-permute-start.2
  10.7 2.5 %collective-permute-start.1 = (bf16[16,2560]{1,0:T(8,128)(2,1)S(1)}, bf16[16,2560]{1,0:T(8,128)(2,1)S(1)}, u32[]{:S(2)}, u32[]{:S(2)}) collective-permute-start(bf16[16,2560]{1,0:T(8,128)(2,1)S(1)} %add_convert_fusion.2), channel_id=1, source_target_pairs={{0,2},{1,7},{2,0},{3,5},{4,6},{5,11},{6,4},{7,9},{8,10},{9,15},{10... | collective-permute-start | bytes 245768 | tf_op jit(solution)/shard_map/ppermute | solution.py:209
  13.2 0.0 collective-permute-start.4
  13.2 1.9 %collective-permute-start.3 = (bf16[16,2560]{1,0:T(8,128)(2,1)S(1)}, bf16[16,2560]{1,0:T(8,128)(2,1)S(1)}, u32[]{:S(2)}, u32[]{:S(2)}) collective-permute-start(bf16[16,2560]{1,0:T(8,128)(2,1)S(1)} %add_convert_fusion.2), channel_id=1, source_target_pairs={{0,1},{1,6},{2,3},{3,4},{4,5},{5,10},{6,7},{7,8},{8,9},{9,14},{10,... | collective-permute-start | bytes 245768 | tf_op jit(solution)/shard_map/ppermute | solution.py:209
  15.2 6.2 %collective-permute-done.2 = bf16[16,2560]{1,0:T(8,128)(2,1)S(1)} collective-permute-done((bf16[16,2560]{1,0:T(8,128)(2,1)S(1)}, bf16[16,2560]{1,0:T(8,128)(2,1)S(1)}, u32[]{:S(2)}, u32[]{:S(2)}) %collective-permute-start.2) | collective-permute-done | bytes 81952 | tf_op jit(solution)/shard_map/ppermute | solution.py:209
  21.4 0.7 %collective-permute-done.1 = bf16[16,2560]{1,0:T(8,128)(2,1)S(1)} collective-permute-done((bf16[16,2560]{1,0:T(8,128)(2,1)S(1)}, bf16[16,2560]{1,0:T(8,128)(2,1)S(1)}, u32[]{:S(2)}, u32[]{:S(2)}) %collective-permute-start.1) | collective-permute-done | bytes 81952 | tf_op jit(solution)/shard_map/ppermute | solution.py:209
  22.1 0.0 collective-permute-done.4
  22.1 0.0 collective-permute-done.3
  22.1 0.7 %fusion.1 = bf16[1,16,2560]{2,1,0:T(8,128)(2,1)} fusion(bf16[16,2560]{1,0:T(8,128)(2,1)S(1)} %collective-permute-done.2, bf16[16,2560]{1,0:T(8,128)(2,1)S(1)} %collective-permute-done.1, bf16[16,2560]{1,0:T(8,128)(2,1)S(1)} %collective-permute-done.4, bf16[16,2560]{1,0:T(8,128)(2,1)S(1)} %collective-permute-done.3, pred[]{:T(512)S(6)} %eq.5), kind=kLoop, calls=%fused_computation.4 | loop fusion | flops 368640 | bytes 409601 | tf_op jit(solution)/shard_map/broadcast_in_dim | solution.py:217
  (1 shorter events, 0.0 us)
Async XLA Ops:
  6.3 4.3 %collective-permute-start = (bf16[16,2560]{1,0:T(8,128)(2,1)S(1)}, bf16[16,2560]{1,0:T(8,128)(2,1)S(1)}, u32[]{:S(2)}, u32[]{:S(2)}) collective-permute-start(bf16[16,2560]{1,0:T(8,128)(2,1)S(1)} %get-tuple-element.6), channel_id=1, source_target_pairs={{0,1},{1,0},{2,3},{3,2},{4,5},{5,4},{6,7},{7,6},{8,9},{9,8},{10,11... | collective-permute-start | bytes 245768 | tf_op jit(solution)/shard_map/ppermute | solution.py:209
  10.6 10.7 %collective-permute-start.2 = (bf16[16,2560]{1,0:T(8,128)(2,1)S(1)}, bf16[16,2560]{1,0:T(8,128)(2,1)S(1)}, u32[]{:S(2)}, u32[]{:S(2)}) collective-permute-start(bf16[16,2560]{1,0:T(8,128)(2,1)S(1)} %add_convert_fusion.2), channel_id=1, source_target_pairs={{0,2},{1,5},{2,0},{3,7},{4,6},{5,9},{6,4},{7,11},{8,10},{9,13},{10... | collective-permute-start | bytes 245768 | tf_op jit(solution)/shard_map/ppermute | solution.py:209
  10.7 11.4 %collective-permute-start.1 = (bf16[16,2560]{1,0:T(8,128)(2,1)S(1)}, bf16[16,2560]{1,0:T(8,128)(2,1)S(1)}, u32[]{:S(2)}, u32[]{:S(2)}) collective-permute-start(bf16[16,2560]{1,0:T(8,128)(2,1)S(1)} %add_convert_fusion.2), channel_id=1, source_target_pairs={{0,2},{1,7},{2,0},{3,5},{4,6},{5,11},{6,4},{7,9},{8,10},{9,15},{10... | collective-permute-start | bytes 245768 | tf_op jit(solution)/shard_map/ppermute | solution.py:209
  13.2 8.8 %collective-permute-start.4 = (bf16[16,2560]{1,0:T(8,128)(2,1)S(1)}, bf16[16,2560]{1,0:T(8,128)(2,1)S(1)}, u32[]{:S(2)}, u32[]{:S(2)}) collective-permute-start(bf16[16,2560]{1,0:T(8,128)(2,1)S(1)} %add_convert_fusion.2), channel_id=1, source_target_pairs={{0,1},{1,4},{2,3},{3,6},{4,5},{5,8},{6,7},{7,10},{8,9},{9,12},{10,... | collective-permute-start | bytes 245768 | tf_op jit(solution)/shard_map/ppermute | solution.py:209
  13.2 8.8 %collective-permute-start.3 = (bf16[16,2560]{1,0:T(8,128)(2,1)S(1)}, bf16[16,2560]{1,0:T(8,128)(2,1)S(1)}, u32[]{:S(2)}, u32[]{:S(2)}) collective-permute-start(bf16[16,2560]{1,0:T(8,128)(2,1)S(1)} %add_convert_fusion.2), channel_id=1, source_target_pairs={{0,1},{1,6},{2,3},{3,4},{4,5},{5,10},{6,7},{7,8},{8,9},{9,14},{10,... | collective-permute-start | bytes 245768 | tf_op jit(solution)/shard_map/ppermute | solution.py:209

commit v3 on v2

--- a/solution.py
+++ b/solution.py
@@ -30,14 +30,14 @@
     slots = ckey.shape[1]
     cached = rows * slots
     heads = wq.shape[2] // HD
-    blocks = wq_sem.shape[0]
+    blocks = BLOCKS
     group = heads // blocks
     span = group * HD
     last = (((1,), (1,)), ((), ()))
 
-    def copy(src, dst, s):
+    def copy(src, dst, s, priority=0):
         c = pltpu.make_async_copy(src, dst, s)
-        c.start()
+        c.start(priority=priority)
         return c
 
     c_state = copy(state, state_v, sem.at[0])
@@ -50,12 +50,12 @@
     c_key = copy(ckey, key_v, sem.at[7])
     c_val = copy(cval, val_v, sem.at[8])
     c_wq = [copy(wq.at[0, :, pl.ds(i * span, span)], wq_v.at[i], wq_sem.at[i]) for i in range(blocks)]
-    c_wo = []
-
-    def start_wo():
-        i = len(c_wo)
+
+    def fetch_wo(i):
         at = pl.ds(i * span, span)
-        c_wo.append(copy(wo.at[0, at], wo_v.at[at], wo_sem.at[i]))
+        return copy(wo.at[0, at], wo_v.at[at], wo_sem.at[i], 1)
+
+    c_wo = [fetch_wo(0)]
 
     c_lens.wait()
     c_state.wait()
@@ -93,6 +93,7 @@
 
     c_wk.wait()
     c_wv.wait()
+    c_wo.extend(fetch_wo(i) for i in range(1, blocks))
     key_value = dot(normed, wkv_v[...])
     new_key = head_norm(key_value[:, :HD], kgain_v[...].astype(F32))
     new_value = key_value[:, HD:].astype(BF16)
@@ -120,21 +121,18 @@
     first = lax.axis_index("tensor") == 0
     out = jnp.where(first, hidden, 0.0)
     c_wq[0].wait()
-    start_wo()
     c_key.wait()
     c_val.wait()
     query = dot(normed, wq_v[0])
     attended = []
     for i in range(1, blocks):
         c_wq[i].wait()
-        start_wo()
         following = dot(normed, wq_v[i])
         attended.append(attend(query))
         query = following
+    attended.append(attend(query))
     for i in range(blocks):
         c_wo[i].wait()
-        if i == 0:
-            attended.append(attend(query))
         out = out + dot(attended[i], wo_v[i * span : (i + 1) * span])
     part[...] = out.astype(BF16)
     c_newk.wait()

time: 22.9 us -> 22.5 us (0.983)
  Pallas kernels: 5.69 us -> 5.37 us
    pallas_call x1, Pallas kernels: 5.69 us -> 5.37 us  [section_partial(): pl.pallas_call(kernel, out_shape=(pltpu.VMEM((rows, width), BF16), pltpu....]
where the time goes in v3:
time: 22.5 us; the launch traced here: 22.4 us
  starting transfers between devices  7.87 us (35%)
  waiting for transfers between devices  7.83 us (35%)
  Pallas kernels  5.37 us (24%)
  other arithmetic  0.7 us (3%)
  between operations  0.66 us (3%)
    ppermute x5, starting transfers between devices, moved(): return lax.ppermute(x, ('section', 'tensor'), pairs)  7.87 us
    ppermute x5, waiting for transfers between devices, moved(): return lax.ppermute(x, ('section', 'tensor'), pairs)  7.83 us
    pallas_call x1, Pallas kernels, section_partial(): pl.pallas_call(kernel, out_shape=(pltpu.VMEM((rows, width), BF16), pltpu....  5.37 us
    broadcast_in_dim x1, other arithmetic, body(): handed[None]  0.68 us
  transfers between devices with their start and end apart: 5, of which 3 were waited for; matrix products, arithmetic and copies ran while one was open for 0% of the time, Pallas kernels for 0%

profile of v3, /device:TPU:1, one launch (start us, length us, event | category | flops | bytes accessed | tf_op | source)
XLA Modules:
  0.0 22.4 jit_solution(10589764693894522894)
XLA Ops:
  0.6 5.4 %shard_map.130 = (bf16[16,2560]{1,0:T(8,128)(2,1)S(1)}, bf16[16,128]{1,0:T(8,128)(2,1)}, bf16[16,128]{1,0:T(8,128)(2,1)}) custom-call(bf16[1,16,2560]{2,1,0:T(8,128)(2,1)} %state.1, bf16[1,2560]{1,0:T(2,128)(2,1)} %gain.1, bf16[1,2560,1024]{2,1,0:T(8,128)(2,1)} %wq.1, bf16[1,2560,128]{2,1,0:T(8,128)(2,1)} %wk.1, bf16[1,2560,128]{2,1,0:T(8,128)(2,1)} %wv.1, ...), custom_call_target="tpu_custom_call" | custom-call | flops 188743680 | bytes 12058624 | tf_op jit(solution)/shard_map/pallas_call | solution.py:152
  6.0 3.3 %collective-permute-start = (bf16[16,2560]{1,0:T(8,128)(2,1)S(1)}, bf16[16,2560]{1,0:T(8,128)(2,1)S(1)}, u32[]{:S(2)}, u32[]{:S(2)}) collective-permute-start(bf16[16,2560]{1,0:T(8,128)(2,1)S(1)} %get-tuple-element.6), channel_id=1, source_target_pairs={{0,1},{1,0},{2,3},{3,2},{4,5},{5,4},{6,7},{7,6},{8,9},{9,8},{10,11... | collective-permute-start | bytes 245768 | tf_op jit(solution)/shard_map/ppermute | solution.py:207
  9.3 0.9 %collective-permute-done = bf16[16,2560]{1,0:T(8,128)(2,1)S(1)} collective-permute-done((bf16[16,2560]{1,0:T(8,128)(2,1)S(1)}, bf16[16,2560]{1,0:T(8,128)(2,1)S(1)}, u32[]{:S(2)}, u32[]{:S(2)}) %collective-permute-start) | collective-permute-done | bytes 81952 | tf_op jit(solution)/shard_map/ppermute | solution.py:207
  10.3 0.1 collective-permute-start.2
  10.4 2.5 %collective-permute-start.1 = (bf16[16,2560]{1,0:T(8,128)(2,1)S(1)}, bf16[16,2560]{1,0:T(8,128)(2,1)S(1)}, u32[]{:S(2)}, u32[]{:S(2)}) collective-permute-start(bf16[16,2560]{1,0:T(8,128)(2,1)S(1)} %add_convert_fusion.2), channel_id=1, source_target_pairs={{0,2},{1,7},{2,0},{3,5},{4,6},{5,11},{6,4},{7,9},{8,10},{9,15},{10... | collective-permute-start | bytes 245768 | tf_op jit(solution)/shard_map/ppermute | solution.py:207
  12.9 0.0 collective-permute-start.4
  12.9 1.9 %collective-permute-start.3 = (bf16[16,2560]{1,0:T(8,128)(2,1)S(1)}, bf16[16,2560]{1,0:T(8,128)(2,1)S(1)}, u32[]{:S(2)}, u32[]{:S(2)}) collective-permute-start(bf16[16,2560]{1,0:T(8,128)(2,1)S(1)} %add_convert_fusion.2), channel_id=1, source_target_pairs={{0,1},{1,6},{2,3},{3,4},{4,5},{5,10},{6,7},{7,8},{8,9},{9,14},{10,... | collective-permute-start | bytes 245768 | tf_op jit(solution)/shard_map/ppermute | solution.py:207
  14.8 6.2 %collective-permute-done.2 = bf16[16,2560]{1,0:T(8,128)(2,1)S(1)} collective-permute-done((bf16[16,2560]{1,0:T(8,128)(2,1)S(1)}, bf16[16,2560]{1,0:T(8,128)(2,1)S(1)}, u32[]{:S(2)}, u32[]{:S(2)}) %collective-permute-start.2) | collective-permute-done | bytes 81952 | tf_op jit(solution)/shard_map/ppermute | solution.py:207
  21.0 0.7 %collective-permute-done.1 = bf16[16,2560]{1,0:T(8,128)(2,1)S(1)} collective-permute-done((bf16[16,2560]{1,0:T(8,128)(2,1)S(1)}, bf16[16,2560]{1,0:T(8,128)(2,1)S(1)}, u32[]{:S(2)}, u32[]{:S(2)}) %collective-permute-start.1) | collective-permute-done | bytes 81952 | tf_op jit(solution)/shard_map/ppermute | solution.py:207
  21.7 0.0 collective-permute-done.4
  21.7 0.0 collective-permute-done.3
  21.7 0.7 %fusion.1 = bf16[1,16,2560]{2,1,0:T(8,128)(2,1)} fusion(bf16[16,2560]{1,0:T(8,128)(2,1)S(1)} %collective-permute-done.2, bf16[16,2560]{1,0:T(8,128)(2,1)S(1)} %collective-permute-done.1, bf16[16,2560]{1,0:T(8,128)(2,1)S(1)} %collective-permute-done.4, bf16[16,2560]{1,0:T(8,128)(2,1)S(1)} %collective-permute-done.3, pred[]{:T(512)S(6)} %eq.5), kind=kLoop, calls=%fused_computation.4 | loop fusion | flops 368640 | bytes 409601 | tf_op jit(solution)/shard_map/broadcast_in_dim | solution.py:215
  (1 shorter events, 0.0 us)
Async XLA Ops:
  6.0 4.3 %collective-permute-start = (bf16[16,2560]{1,0:T(8,128)(2,1)S(1)}, bf16[16,2560]{1,0:T(8,128)(2,1)S(1)}, u32[]{:S(2)}, u32[]{:S(2)}) collective-permute-start(bf16[16,2560]{1,0:T(8,128)(2,1)S(1)} %get-tuple-element.6), channel_id=1, source_target_pairs={{0,1},{1,0},{2,3},{3,2},{4,5},{5,4},{6,7},{7,6},{8,9},{9,8},{10,11... | collective-permute-start | bytes 245768 | tf_op jit(solution)/shard_map/ppermute | solution.py:207
  10.3 10.7 %collective-permute-start.2 = (bf16[16,2560]{1,0:T(8,128)(2,1)S(1)}, bf16[16,2560]{1,0:T(8,128)(2,1)S(1)}, u32[]{:S(2)}, u32[]{:S(2)}) collective-permute-start(bf16[16,2560]{1,0:T(8,128)(2,1)S(1)} %add_convert_fusion.2), channel_id=1, source_target_pairs={{0,2},{1,5},{2,0},{3,7},{4,6},{5,9},{6,4},{7,11},{8,10},{9,13},{10... | collective-permute-start | bytes 245768 | tf_op jit(solution)/shard_map/ppermute | solution.py:207
  10.4 11.4 %collective-permute-start.1 = (bf16[16,2560]{1,0:T(8,128)(2,1)S(1)}, bf16[16,2560]{1,0:T(8,128)(2,1)S(1)}, u32[]{:S(2)}, u32[]{:S(2)}) collective-permute-start(bf16[16,2560]{1,0:T(8,128)(2,1)S(1)} %add_convert_fusion.2), channel_id=1, source_target_pairs={{0,2},{1,7},{2,0},{3,5},{4,6},{5,11},{6,4},{7,9},{8,10},{9,15},{10... | collective-permute-start | bytes 245768 | tf_op jit(solution)/shard_map/ppermute | solution.py:207
  12.9 8.8 %collective-permute-start.4 = (bf16[16,2560]{1,0:T(8,128)(2,1)S(1)}, bf16[16,2560]{1,0:T(8,128)(2,1)S(1)}, u32[]{:S(2)}, u32[]{:S(2)}) collective-permute-start(bf16[16,2560]{1,0:T(8,128)(2,1)S(1)} %add_convert_fusion.2), channel_id=1, source_target_pairs={{0,1},{1,4},{2,3},{3,6},{4,5},{5,8},{6,7},{7,10},{8,9},{9,12},{10,... | collective-permute-start | bytes 245768 | tf_op jit(solution)/shard_map/ppermute | solution.py:207
  12.9 8.8 %collective-permute-start.3 = (bf16[16,2560]{1,0:T(8,128)(2,1)S(1)}, bf16[16,2560]{1,0:T(8,128)(2,1)S(1)}, u32[]{:S(2)}, u32[]{:S(2)}) collective-permute-start(bf16[16,2560]{1,0:T(8,128)(2,1)S(1)} %add_convert_fusion.2), channel_id=1, source_target_pairs={{0,1},{1,6},{2,3},{3,4},{4,5},{5,10},{6,7},{7,8},{8,9},{9,14},{10,... | collective-permute-start | bytes 245768 | tf_op jit(solution)/shard_map/ppermute | solution.py:207

commit v4 on v3

--- a/solution.py
+++ b/solution.py
@@ -131,10 +131,14 @@
         attended.append(attend(query))
         query = following
     attended.append(attend(query))
-    for i in range(blocks):
-        c_wo[i].wait()
-        out = out + dot(attended[i], wo_v[i * span : (i + 1) * span])
-    part[...] = out.astype(BF16)
+    c_wo[0].wait()
+    outs = []
+    for at in range(0, width, 512):
+        outs.append(out[:, at : at + 512] + dot(attended[0], wo_v[:span, at : at + 512]))
+    c_wo[1].wait()
+    for k, at in enumerate(range(0, width, 512)):
+        share = dot(attended[1], wo_v[span:, at : at + 512])
+        part[:, at : at + 512] = (outs[k] + share).astype(BF16)
     c_newk.wait()
     c_newv.wait()
 

time: 22.5 us -> 22.5 us (level)
  no operation moved by 1% of the time
where the time goes in v4:
time: 22.5 us; the launch traced here: 22.4 us
  starting transfers between devices  7.87 us (35%)
  waiting for transfers between devices  7.83 us (35%)
  Pallas kernels  5.37 us (24%)
  other arithmetic  0.7 us (3%)
  between operations  0.66 us (3%)
    ppermute x5, starting transfers between devices, moved(): return lax.ppermute(x, ('section', 'tensor'), pairs)  7.87 us
    ppermute x5, waiting for transfers between devices, moved(): return lax.ppermute(x, ('section', 'tensor'), pairs)  7.83 us
    pallas_call x1, Pallas kernels, section_partial(): pl.pallas_call(kernel, out_shape=(pltpu.VMEM((rows, width), BF16), pltpu....  5.37 us
    broadcast_in_dim x1, other arithmetic, body(): handed[None]  0.68 us
  transfers between devices with their start and end apart: 5, of which 3 were waited for; matrix products, arithmetic and copies ran while one was open for 0% of the time, Pallas kernels for 0%

profile of v4, /device:TPU:1, one launch (start us, length us, event | category | flops | bytes accessed | tf_op | source)
XLA Modules:
  0.0 22.4 jit_solution(10589764693894522894)
XLA Ops:
  0.6 5.4 %shard_map.130 = (bf16[16,2560]{1,0:T(8,128)(2,1)S(1)}, bf16[16,128]{1,0:T(8,128)(2,1)}, bf16[16,128]{1,0:T(8,128)(2,1)}) custom-call(bf16[1,16,2560]{2,1,0:T(8,128)(2,1)} %state.1, bf16[1,2560]{1,0:T(2,128)(2,1)} %gain.1, bf16[1,2560,1024]{2,1,0:T(8,128)(2,1)} %wq.1, bf16[1,2560,128]{2,1,0:T(8,128)(2,1)} %wk.1, bf16[1,2560,128]{2,1,0:T(8,128)(2,1)} %wv.1, ...), custom_call_target="tpu_custom_call" | custom-call | flops 188743680 | bytes 12058624 | tf_op jit(solution)/shard_map/pallas_call | solution.py:156
  6.0 3.3 %collective-permute-start = (bf16[16,2560]{1,0:T(8,128)(2,1)S(1)}, bf16[16,2560]{1,0:T(8,128)(2,1)S(1)}, u32[]{:S(2)}, u32[]{:S(2)}) collective-permute-start(bf16[16,2560]{1,0:T(8,128)(2,1)S(1)} %get-tuple-element.6), channel_id=1, source_target_pairs={{0,1},{1,0},{2,3},{3,2},{4,5},{5,4},{6,7},{7,6},{8,9},{9,8},{10,11... | collective-permute-start | bytes 245768 | tf_op jit(solution)/shard_map/ppermute | solution.py:211
  9.3 0.9 %collective-permute-done = bf16[16,2560]{1,0:T(8,128)(2,1)S(1)} collective-permute-done((bf16[16,2560]{1,0:T(8,128)(2,1)S(1)}, bf16[16,2560]{1,0:T(8,128)(2,1)S(1)}, u32[]{:S(2)}, u32[]{:S(2)}) %collective-permute-start) | collective-permute-done | bytes 81952 | tf_op jit(solution)/shard_map/ppermute | solution.py:211
  10.3 0.1 collective-permute-start.2
  10.4 2.5 %collective-permute-start.1 = (bf16[16,2560]{1,0:T(8,128)(2,1)S(1)}, bf16[16,2560]{1,0:T(8,128)(2,1)S(1)}, u32[]{:S(2)}, u32[]{:S(2)}) collective-permute-start(bf16[16,2560]{1,0:T(8,128)(2,1)S(1)} %add_convert_fusion.2), channel_id=1, source_target_pairs={{0,2},{1,7},{2,0},{3,5},{4,6},{5,11},{6,4},{7,9},{8,10},{9,15},{10... | collective-permute-start | bytes 245768 | tf_op jit(solution)/shard_map/ppermute | solution.py:211
  12.9 0.0 collective-permute-start.4
  12.9 1.9 %collective-permute-start.3 = (bf16[16,2560]{1,0:T(8,128)(2,1)S(1)}, bf16[16,2560]{1,0:T(8,128)(2,1)S(1)}, u32[]{:S(2)}, u32[]{:S(2)}) collective-permute-start(bf16[16,2560]{1,0:T(8,128)(2,1)S(1)} %add_convert_fusion.2), channel_id=1, source_target_pairs={{0,1},{1,6},{2,3},{3,4},{4,5},{5,10},{6,7},{7,8},{8,9},{9,14},{10,... | collective-permute-start | bytes 245768 | tf_op jit(solution)/shard_map/ppermute | solution.py:211
  14.8 6.2 %collective-permute-done.2 = bf16[16,2560]{1,0:T(8,128)(2,1)S(1)} collective-permute-done((bf16[16,2560]{1,0:T(8,128)(2,1)S(1)}, bf16[16,2560]{1,0:T(8,128)(2,1)S(1)}, u32[]{:S(2)}, u32[]{:S(2)}) %collective-permute-start.2) | collective-permute-done | bytes 81952 | tf_op jit(solution)/shard_map/ppermute | solution.py:211
  21.0 0.7 %collective-permute-done.1 = bf16[16,2560]{1,0:T(8,128)(2,1)S(1)} collective-permute-done((bf16[16,2560]{1,0:T(8,128)(2,1)S(1)}, bf16[16,2560]{1,0:T(8,128)(2,1)S(1)}, u32[]{:S(2)}, u32[]{:S(2)}) %collective-permute-start.1) | collective-permute-done | bytes 81952 | tf_op jit(solution)/shard_map/ppermute | solution.py:211
  21.7 0.0 collective-permute-done.4
  21.7 0.0 collective-permute-done.3
  21.7 0.7 %fusion.1 = bf16[1,16,2560]{2,1,0:T(8,128)(2,1)} fusion(bf16[16,2560]{1,0:T(8,128)(2,1)S(1)} %collective-permute-done.2, bf16[16,2560]{1,0:T(8,128)(2,1)S(1)} %collective-permute-done.1, bf16[16,2560]{1,0:T(8,128)(2,1)S(1)} %collective-permute-done.4, bf16[16,2560]{1,0:T(8,128)(2,1)S(1)} %collective-permute-done.3, pred[]{:T(512)S(6)} %eq.5), kind=kLoop, calls=%fused_computation.4 | loop fusion | flops 368640 | bytes 409601 | tf_op jit(solution)/shard_map/broadcast_in_dim | solution.py:219
  (1 shorter events, 0.0 us)
Async XLA Ops:
  6.0 4.3 %collective-permute-start = (bf16[16,2560]{1,0:T(8,128)(2,1)S(1)}, bf16[16,2560]{1,0:T(8,128)(2,1)S(1)}, u32[]{:S(2)}, u32[]{:S(2)}) collective-permute-start(bf16[16,2560]{1,0:T(8,128)(2,1)S(1)} %get-tuple-element.6), channel_id=1, source_target_pairs={{0,1},{1,0},{2,3},{3,2},{4,5},{5,4},{6,7},{7,6},{8,9},{9,8},{10,11... | collective-permute-start | bytes 245768 | tf_op jit(solution)/shard_map/ppermute | solution.py:211
  10.3 10.7 %collective-permute-start.2 = (bf16[16,2560]{1,0:T(8,128)(2,1)S(1)}, bf16[16,2560]{1,0:T(8,128)(2,1)S(1)}, u32[]{:S(2)}, u32[]{:S(2)}) collective-permute-start(bf16[16,2560]{1,0:T(8,128)(2,1)S(1)} %add_convert_fusion.2), channel_id=1, source_target_pairs={{0,2},{1,5},{2,0},{3,7},{4,6},{5,9},{6,4},{7,11},{8,10},{9,13},{10... | collective-permute-start | bytes 245768 | tf_op jit(solution)/shard_map/ppermute | solution.py:211
  10.4 11.4 %collective-permute-start.1 = (bf16[16,2560]{1,0:T(8,128)(2,1)S(1)}, bf16[16,2560]{1,0:T(8,128)(2,1)S(1)}, u32[]{:S(2)}, u32[]{:S(2)}) collective-permute-start(bf16[16,2560]{1,0:T(8,128)(2,1)S(1)} %add_convert_fusion.2), channel_id=1, source_target_pairs={{0,2},{1,7},{2,0},{3,5},{4,6},{5,11},{6,4},{7,9},{8,10},{9,15},{10... | collective-permute-start | bytes 245768 | tf_op jit(solution)/shard_map/ppermute | solution.py:211
  12.9 8.8 %collective-permute-start.4 = (bf16[16,2560]{1,0:T(8,128)(2,1)S(1)}, bf16[16,2560]{1,0:T(8,128)(2,1)S(1)}, u32[]{:S(2)}, u32[]{:S(2)}) collective-permute-start(bf16[16,2560]{1,0:T(8,128)(2,1)S(1)} %add_convert_fusion.2), channel_id=1, source_target_pairs={{0,1},{1,4},{2,3},{3,6},{4,5},{5,8},{6,7},{7,10},{8,9},{9,12},{10,... | collective-permute-start | bytes 245768 | tf_op jit(solution)/shard_map/ppermute | solution.py:211
  12.9 8.8 %collective-permute-start.3 = (bf16[16,2560]{1,0:T(8,128)(2,1)S(1)}, bf16[16,2560]{1,0:T(8,128)(2,1)S(1)}, u32[]{:S(2)}, u32[]{:S(2)}) collective-permute-start(bf16[16,2560]{1,0:T(8,128)(2,1)S(1)} %add_convert_fusion.2), channel_id=1, source_target_pairs={{0,1},{1,6},{2,3},{3,4},{4,5},{5,10},{6,7},{7,8},{8,9},{9,14},{10,... | collective-permute-start | bytes 245768 | tf_op jit(solution)/shard_map/ppermute | solution.py:211
